TPU v7x, 128 devices: a whole 4x4x4 slice. The times are simulated.
128 devices in a mesh: span: 16 (over x_lo, y, core), patch: 8 (over x_hi, z).
Axes of the slice: x: 4 (x_hi: 2, x_lo: 2; x = x_hi * 2 + x_lo), y: 4, z: 4, core: 2. Of those that a mesh axis runs over, the one named last changes fastest.
Arguments:
- queries: bfloat16 [16, 512, 3072], P('span', 'patch'), may hold values from -8 to 8
- keys: bfloat16 [16, 512, 3072], P('span', 'patch'), may hold values from -8 to 8
- values: bfloat16 [16, 512, 3072], P('span', 'patch'), may hold values from -6 to 6
- q_gain: float32 [3072], replicated, may hold values from 0.1 to 1.9
- k_gain: float32 [3072], replicated, may hold values from 0.1 to 1.9
- gate_table: float32 [50, 3072], replicated, may hold values from 0.3 to 1.7
- noise_step: int32 [16], P('span'), may hold values from 0 to 49
- block_mask: int32 [16, 16], replicated, may hold values from 0 to 1, as said below
- finished: int32 [1], replicated, may hold values from 0 to 15
Outputs:
- mixed: bfloat16 [16, 512, 3072], P('span', 'patch')
- committed_k: bfloat16 [512, 3072], P('span', 'patch')
- committed_v: bfloat16 [512, 3072], P('span', 'patch')
Inputs may be any that keep to these rules, and one draw needn't show every extreme that they name: block-causal with a history window: for each span c there is a first span s[c] <= c, and block_mask[c, j] = 1 exactly for s[c] <= j <= c.
All inputs are finite; a program needn't handle non-finite values.
Results may differ from a plain program's by a relative error of at most 0.0085.
Values may be sent and summed in bfloat16 or wider, within the bound.
No kernel may reach another device: no remote copies, remote signals or barrier semaphores. Data moves between devices by JAX's collectives and lax.ppermute only.
A program may use at most 128 MiB of HBM per device.

v0:
```python
import functools

import jax
import jax.numpy as jnp
from jax import lax
from jax.experimental import pallas as pl
from jax.experimental.pallas import tpu as pltpu
from jax.sharding import Mesh
from jax.sharding import PartitionSpec as P

D = 128
HEADS = 24
HD = HEADS * D
SPANS = 16
TOK = 64
HALF = TOK // 2
SLOTS = 32
CHIPS = 2 * SLOTS
ROWS = 2 * TOK + HALF
OUT_ROWS = 2 * HALF
PLANE = ("xl", "y", "xh", "z")
EPS = 1e-06
SCALE = D ** (-0.5)
VMEM = pl.BlockSpec(memory_space=pltpu.VMEM)
SMEM = pl.BlockSpec(memory_space=pltpu.SMEM)


def head_slot():
    return lax.axis_index("y") * 8 + patch_index()


def patch_index():
    return lax.axis_index("xh") * 4 + lax.axis_index("z")


def pack_kernel(q_ref, k_ref, v_ref, q_gain, k_gain, out_ref):
    def factor(ref):
        wide = ref[0].astype(jnp.float32)
        return lax.rsqrt(jnp.mean(wide * wide, axis=-1, keepdims=True) + EPS)

    q_factor = factor(q_ref)
    k_factor = factor(k_ref)
    for h in range(HEADS):
        cols = slice(h * D, (h + 1) * D)
        qn = (q_ref[0, :, cols].astype(jnp.float32) * q_factor * q_gain[:, cols]).astype(jnp.bfloat16)
        kn = (k_ref[0, :, cols].astype(jnp.float32) * k_factor * k_gain[:, cols]).astype(jnp.bfloat16)
        for x in range(2):
            out_ref[x * SLOTS + h, 0:TOK, :] = kn
            out_ref[x * SLOTS + h, TOK : 2 * TOK, :] = v_ref[0, :, cols]
            out_ref[x * SLOTS + h, 2 * TOK : ROWS, :] = qn[x * HALF : (x + 1) * HALF]


def attend_kernel(mask_ref, fin_ref, own_ref, peer_ref, out_ref):
    core = lax.axis_index("core")
    xl = lax.axis_index("xl")
    head = head_slot()

    def block(q, ref, u, state):
        most, total, summed = state
        k = ref[pl.ds(u * 8, 8), 0:TOK, :].reshape(8 * TOK, D)
        v = ref[pl.ds(u * 8, 8), TOK : 2 * TOK, :].reshape(8 * TOK, D)
        scores = lax.dot_general(q, k, (((1,), (1,)), ((), ())), preferred_element_type=jnp.float32) * SCALE
        newest = jnp.maximum(most, jnp.max(scores, axis=1, keepdims=True))
        weight = jnp.exp(scores - newest)
        factor = jnp.exp(most - newest)
        part = weight[:, 0:D]
        for i in range(1, 4):
            part = part + weight[:, i * D : (i + 1) * D]
        total = total * factor + part
        added = jnp.dot(weight.astype(jnp.bfloat16), v, preferred_element_type=jnp.float32)
        return newest, total, summed * factor + added

    @pl.when(head < HEADS)
    def _():
        def span(t, carry):
            c = 2 * t + core
            counted = mask_ref[c, 0]
            for j in range(1, SPANS):
                counted = counted + mask_ref[c, j]
            first = c + 1 - counted
            q = own_ref[pl.ds(t * 8, 8), 2 * TOK : ROWS, :].reshape(8 * HALF, D)
            state = (
                jnp.full((8 * HALF, 1), -1e30, jnp.float32),
                jnp.zeros((8 * HALF, D), jnp.float32),
                jnp.zeros((8 * HALF, D), jnp.float32),
            )
            state = lax.fori_loop(
                (first - core + 1) // 2, t + 1, lambda u, s: block(q, own_ref, u, s), state
            )
            state = lax.fori_loop(
                (first + core) // 2, t + core, lambda u, s: block(q, peer_ref, u, s), state
            )
            _, total, summed = state
            attn = summed / jnp.sum(total, axis=1, keepdims=True)
            out_ref[pl.ds(t * 8, 8), 0:HALF, :] = attn.astype(jnp.bfloat16).reshape(8, HALF, D)
            return carry

        lax.fori_loop(0, 8, span, 0)

        fin = fin_ref[0]
        column = head // 3
        start = core * HALF + xl * (HALF // 2)

        def commit(ref):
            for t in range(8):
                slot = (fin // 2) * 8 + t
                for i in range(2):
                    rows = ref[slot, pl.ds(pl.multiple_of(start + i * TOK, 16), HALF // 2), :]
                    out_ref[t * 8 + column, pl.ds(HALF + i * (HALF // 2), HALF // 2), :] = rows

        pl.when(fin % 2 == core)(lambda: commit(own_ref))
        pl.when(fin % 2 != core)(lambda: commit(peer_ref))


def finish_kernel(step_ref, in_ref, gate_ref, mixed_ref, k_ref, v_ref):
    gate = gate_ref[pl.ds(step_ref[0], 1), :]
    for h in range(HEADS):
        cols = slice(h * D, (h + 1) * D)
        for x in range(2):
            rows = slice(x * HALF, (x + 1) * HALF)
            attn = in_ref[x * SLOTS + h, 0:HALF, :].astype(jnp.float32)
            mixed_ref[0, rows, cols] = (attn * gate[:, cols]).astype(jnp.bfloat16)
    patch = patch_index()
    for i in range(3):
        for x in range(2):
            src = x * SLOTS + 3 * patch + i
            rows = slice(x * (HALF // 2), (x + 1) * (HALF // 2))
            k_ref[rows, i * D : (i + 1) * D] = in_ref[src, HALF : HALF + HALF // 2, :]
            v_ref[rows, i * D : (i + 1) * D] = in_ref[src, HALF + HALF // 2 : OUT_ROWS, :]


PARAMS = pltpu.CompilerParams(vmem_limit_bytes=40 * 1024 * 1024)


def on_device(queries, keys, values, q_gain, k_gain, gate_table, noise_step, block_mask, finished):
    bf16 = jnp.bfloat16
    packed = pl.pallas_call(
        pack_kernel,
        out_shape=jax.ShapeDtypeStruct((CHIPS, ROWS, D), bf16),
        in_specs=[VMEM] * 5,
        out_specs=VMEM,
        compiler_params=PARAMS,
    )(queries, keys, values, q_gain.reshape(1, HD), k_gain.reshape(1, HD))
    own = lax.all_to_all(packed, PLANE, 0, 0, tiled=True)
    peer = lax.ppermute(own, "core", [(0, 1), (1, 0)])
    outs = pl.pallas_call(
        attend_kernel,
        out_shape=jax.ShapeDtypeStruct((CHIPS, OUT_ROWS, D), bf16),
        in_specs=[SMEM, SMEM, VMEM, VMEM],
        out_specs=VMEM,
        compiler_params=PARAMS,
    )(block_mask, finished, own, peer)
    back = lax.all_to_all(outs, PLANE, 0, 0, tiled=True)
    return pl.pallas_call(
        finish_kernel,
        out_shape=(
            jax.ShapeDtypeStruct((1, TOK, HD), bf16),
            jax.ShapeDtypeStruct((HALF, 3 * D), bf16),
            jax.ShapeDtypeStruct((HALF, 3 * D), bf16),
        ),
        in_specs=[SMEM, VMEM, VMEM],
        out_specs=(VMEM, VMEM, VMEM),
        compiler_params=PARAMS,
    )(noise_step, back, gate_table)


def solution(mesh):
    fine = Mesh(mesh.devices.reshape(2, 4, 2, 2, 4), ("xl", "y", "core", "xh", "z"))
    span, patch = ("xl", "y", "core"), ("xh", "z")
    rows = P(span, patch, None)
    return jax.shard_map(
        on_device,
        mesh=fine,
        in_specs=(rows, rows, rows, P(), P(), P(), P(span), P(), P()),
        out_specs=(rows, P(span, patch), P(span, patch)),
        check_vma=False,
    )
```

profile of v0, /device:TPU:1, one launch (start us, length us, event | category | flops | bytes accessed | tf_op | source)
XLA Modules:
  0.0 107.9 jit_solution(8503074790808901055)
XLA Ops:
  0.6 0.0 copy-start.1
  0.6 1.0 copy-done.1
  1.6 0.0 copy-start.2
  1.6 1.0 copy-done.2
  2.6 0.0 copy-start.3
  2.6 1.0 copy-done.3
  3.6 0.0 copy-start.4
  3.6 0.7 copy-done.4
  4.3 0.0 copy-start.5
  4.3 0.7 copy-done.5
  5.0 0.4 shard_map.112
  5.4 0.0 copy-start.6
  5.4 46.5 %all_to_all.10.own_ref = bf16[64,160,128]{2,1,0:T(8,128)(2,1)S(1)} all-to-all(bf16[64,160,128]{2,1,0:T(8,128)(2,1)S(1)} %shard_map.112), channel_id=1, replica_groups=mesh['xl'=2,'y'=4,'core'=2,'xh'=2,'z'=4] {'xl','y','xh','z'}, dimensions={0} | all-to-all | bytes 5242880 | tf_op jit(solution)/shard_map/all_to_all | solution.py:144
  52.0 2.6 %collective-permute-start = (bf16[64,160,128]{2,1,0:T(8,128)(2,1)S(1)}, bf16[64,160,128]{2,1,0:T(8,128)(2,1)S(1)}, u32[]{:S(2)}, u32[]{:S(2)}) collective-permute-start(bf16[64,160,128]{2,1,0:T(8,128)(2,1)S(1)} %all_to_all.10.own_ref), channel_id=1, source_target_pairs={{0,8},{8,0},{1,9},{9,1},{2,10},{10,2},{3,11},{11,3},{4,12},{12,4},... | collective-permute-start | bytes 7864328 | tf_op jit(solution)/shard_map/ppermute | solution.py:145
  55.2 0.0 copy-start
  55.2 3.9 %collective-permute-done.peer_ref = bf16[64,160,128]{2,1,0:T(8,128)(2,1)S(1)} collective-permute-done((bf16[64,160,128]{2,1,0:T(8,128)(2,1)S(1)}, bf16[64,160,128]{2,1,0:T(8,128)(2,1)S(1)}, u32[]{:S(2)}, u32[]{:S(2)}) %collective-permute-start) | collective-permute-done | bytes 2621472 | tf_op jit(solution)/shard_map/ppermute | solution.py:145
  59.1 0.0 copy-done.6
  59.1 27.2 %shard_map.113 = bf16[64,64,128]{2,1,0:T(8,128)(2,1)} custom-call(s32[16,16]{1,0:T(8,128)S(1)} %copy-done.6, s32[1]{0:T(128)S(6)} %copy.13.fin_ref, bf16[64,160,128]{2,1,0:T(8,128)(2,1)S(1)} %all_to_all.10.own_ref, bf16[64,160,128]{2,1,0:T(8,128)(2,1)S(1)} %collective-permute-done.peer_ref), custom_call_target="tpu_custom_call" | custom-call | tf_op jit(solution)/shard_map/pallas_call | solution.py:146
  86.3 4.9 %all-to-all-start.1 = ((bf16[64,64,128]{2,1,0:T(8,128)(2,1)}), bf16[64,64,128]{2,1,0:T(8,128)(2,1)S(1)}, u32[]{:S(2)}, u32[]{:S(2)}) async-start(bf16[64,64,128]{2,1,0:T(8,128)(2,1)} %shard_map.113), calls=%async_computation.1 | async-start | bytes 2097152 | tf_op jit(solution)/shard_map/all_to_all | solution.py:153
  91.9 15.2 %all-to-all-done.1.in_ref = bf16[64,64,128]{2,1,0:T(8,128)(2,1)S(1)} async-done(((bf16[64,64,128]{2,1,0:T(8,128)(2,1)}), bf16[64,64,128]{2,1,0:T(8,128)(2,1)S(1)}, u32[]{:S(2)}, u32[]{:S(2)}) %all-to-all-start.1) | async-done | bytes 1048608 | tf_op jit(solution)/shard_map/all_to_all | solution.py:153
  107.1 0.0 copy-done
  107.1 0.8 shard_map.114
Async XLA Ops:
  0.6 1.0 copy-start.1
  1.6 1.0 copy-start.2
  2.6 1.0 copy-start.3
  3.6 0.7 copy-start.4
  4.3 0.7 copy-start.5
  5.4 53.7 %copy-start.6 = (s32[16,16]{1,0:T(8,128)S(1)}, s32[16,16]{1,0:T(8,128)}, u32[]{:S(2)}) copy-start(s32[16,16]{1,0:T(8,128)} %mask_ref.1) | copy-start | bytes 3076
  52.0 7.1 %collective-permute-start = (bf16[64,160,128]{2,1,0:T(8,128)(2,1)S(1)}, bf16[64,160,128]{2,1,0:T(8,128)(2,1)S(1)}, u32[]{:S(2)}, u32[]{:S(2)}) collective-permute-start(bf16[64,160,128]{2,1,0:T(8,128)(2,1)S(1)} %all_to_all.10.own_ref), channel_id=1, source_target_pairs={{0,8},{8,0},{1,9},{9,1},{2,10},{10,2},{3,11},{11,3},{4,12},{12,4},... | collective-permute-start | bytes 7864328 | tf_op jit(solution)/shard_map/ppermute | solution.py:145
  55.2 51.9 %copy-start = (f32[50,3072]{1,0:T(8,128)S(1)}, f32[50,3072]{1,0:T(8,128)}, u32[]{:S(2)}) copy-start(f32[50,3072]{1,0:T(8,128)} %gate_ref.1) | copy-start | bytes 1843204
  86.3 20.8 %all-to-all-start.1 = ((bf16[64,64,128]{2,1,0:T(8,128)(2,1)}), bf16[64,64,128]{2,1,0:T(8,128)(2,1)S(1)}, u32[]{:S(2)}, u32[]{:S(2)}) async-start(bf16[64,64,128]{2,1,0:T(8,128)(2,1)} %shard_map.113), calls=%async_computation.1 | async-start | bytes 2097152 | tf_op jit(solution)/shard_map/all_to_all | solution.py:153
where the time goes:
time: 109 us; the launch traced here: 108 us
  blocking collectives  46.5 us (43%)
  Pallas kernels  28.4 us (26%)
  waiting for transfers between devices  19.1 us (18%)
  starting transfers between devices  7.5 us (7%)
  local copies, waits for them, and re-layouts  4.4 us (4%)
  between operations  1.97 us (2%)
    all_to_all x1, blocking collectives, on_device(): own = lax.all_to_all(packed, PLANE, 0, 0, tiled=True)  46.5 us
    pallas_call x1, Pallas kernels, on_device(): pl.pallas_call(attend_kernel, out_shape=jax.ShapeDtypeStruct((CHIPS, OUT_...  27.2 us
    all_to_all x1, waiting for transfers between devices, on_device(): back = lax.all_to_all(outs, PLANE, 0, 0, tiled=True)  15.2 us
    all_to_all x1, starting transfers between devices, on_device(): back = lax.all_to_all(outs, PLANE, 0, 0, tiled=True)  4.91 us
    unnamed x14, local copies, waits for them, and re-layouts  4.4 us
    ppermute x1, waiting for transfers between devices, on_device(): peer = lax.ppermute(own, 'core', [(0, 1), (1, 0)])  3.87 us
    ppermute x1, starting transfers between devices, on_device(): peer = lax.ppermute(own, 'core', [(0, 1), (1, 0)])  2.58 us
  transfers between devices with their start and end apart: 2, of which 2 were waited for; matrix products, arithmetic and copies ran while one was open for 0% of the time, Pallas kernels for 0%

commit v1 on v0

v1 whole, which is shorter than its diff:
```python
import math

import jax
import jax.numpy as jnp
from jax import lax
from jax.experimental import pallas as pl
from jax.experimental.pallas import tpu as pltpu
from jax.sharding import Mesh
from jax.sharding import PartitionSpec as P

D = 128
HEADS = 24
HD = HEADS * D
SPANS = 16
TOK = 64
HALF = TOK // 2
SLOTS = 32
CHIPS = 2 * SLOTS
ROWS = 2 * TOK + HALF
OUT_ROWS = 2 * HALF
PLANE = ("xl", "y", "xh", "z")
EPS = 1e-06
SCALE = D ** (-0.5)
SCALE_LOG2 = SCALE * math.log2(math.e)
Q_ROWS = 8 * HALF
BATCH = 4
LEAST, LARGEST = 2.0**-60, 2.0**100
NT = (((1,), (1,)), ((), ()))
VMEM = pl.BlockSpec(memory_space=pltpu.VMEM)
HBM = pl.BlockSpec(memory_space=pltpu.HBM)
SMEM = pl.BlockSpec(memory_space=pltpu.SMEM)


def head_slot():
    return lax.axis_index("y") * 8 + patch_index()


def patch_index():
    return lax.axis_index("xh") * 4 + lax.axis_index("z")


def pack_kernel(q_hbm, k_hbm, v_hbm, qg_hbm, kg_hbm, out_ref, q_ref, k_ref, v_ref, q_gain, k_gain, sems):
    copies = [
        pltpu.make_async_copy(src, dst, sems.at[i])
        for i, (src, dst) in enumerate(
            ((q_hbm, q_ref), (k_hbm, k_ref), (v_hbm, v_ref), (qg_hbm, q_gain), (kg_hbm, k_gain))
        )
    ]
    for copy in copies:
        copy.start()

    def factor(ref):
        wide = ref[0].astype(jnp.float32)
        return lax.rsqrt(jnp.mean(wide * wide, axis=-1, keepdims=True) + EPS)

    def normed(ref, scale, gain, h):
        wide = ref[0, :, h * D : (h + 1) * D].astype(jnp.float32)
        return (wide * scale * gain[h : h + 1, :]).astype(jnp.bfloat16)

    copies[0].wait()
    q_factor = factor(q_ref)
    copies[1].wait()
    k_factor = factor(k_ref)
    for copy in copies[2:]:
        copy.wait()
    for h in range(HEADS):
        qn = normed(q_ref, q_factor, q_gain, h)
        kn = normed(k_ref, k_factor, k_gain, h)
        for x in range(2):
            out_ref[x * SLOTS + h, 0:TOK, :] = kn
            out_ref[x * SLOTS + h, TOK : 2 * TOK, :] = v_ref[0, :, h * D : (h + 1) * D]
            out_ref[x * SLOTS + h, 2 * TOK : ROWS, :] = qn[x * HALF : (x + 1) * HALF]


def q_rows(ref, t):
    return ref[pl.ds(t * 8, 8), 2 * TOK : ROWS, :].reshape(Q_ROWS, D)


def span_keys(ref, u):
    return ref[pl.ds(u * 8, 8), 0:TOK, :].reshape(8 * TOK, D)


def span_values(ref, u):
    return ref[pl.ds(u * 8, 8), TOK : 2 * TOK, :].reshape(8 * TOK, D)


def first_counted(mask_ref, c):
    counted = mask_ref[c, 0]
    for j in range(1, SPANS):
        counted = counted + mask_ref[c, j]
    return c + 1 - counted


def own_range(mask_ref, core, t):
    first = first_counted(mask_ref, 2 * t + core)
    return (first - core + 1) // 2, t + 1


def peer_range(mask_ref, core, t):
    first = first_counted(mask_ref, 2 * t + core)
    return (first + core) // 2, t + core


def accumulate(bounds, q_ref, kv_ref, acc_ref, tot_ref, list_ref):
    n = jnp.int32(0)
    for t in range(8):
        low, high = bounds(t)

        def note(u, at, t=t):
            list_ref[0, at] = t
            list_ref[1, at] = t
            list_ref[2, at] = u
            return at + 1

        n = lax.fori_loop(low, high, note, n)
    for i in range(BATCH - 1):
        list_ref[0, n + i] = 0
        list_ref[1, n + i] = 8
        list_ref[2, n + i] = 0

    def batch(b, carry):
        for i in range(BATCH):
            at = b * BATCH + i
            u = list_ref[2, at]
            scores = lax.dot_general(
                q_rows(q_ref, list_ref[0, at]), span_keys(kv_ref, u), NT, preferred_element_type=jnp.float32
            )
            weight = jnp.exp2(scores * SCALE_LOG2)
            part = weight[:, 0:D]
            for k in range(1, 4):
                part = part + weight[:, k * D : (k + 1) * D]
            added = jnp.dot(weight.astype(jnp.bfloat16), span_values(kv_ref, u), preferred_element_type=jnp.float32)
            row = list_ref[1, at]
            acc_ref[row] += added
            tot_ref[row] += part
        return carry

    lax.fori_loop(0, (n + BATCH - 1) // BATCH, batch, 0)


def own_kernel(mask_ref, own_ref, acc_ref, tot_ref, list_ref):
    core = lax.axis_index("core")

    @pl.when(head_slot() < HEADS)
    def _():
        acc_ref[...] = jnp.zeros_like(acc_ref)
        tot_ref[...] = jnp.zeros_like(tot_ref)
        accumulate(lambda t: own_range(mask_ref, core, t), own_ref, own_ref, acc_ref, tot_ref, list_ref)


def peer_kernel(mask_ref, fin_ref, own_ref, peer_ref, acc_in, tot_in, out_ref, acc_ref, tot_ref, list_ref):
    core = lax.axis_index("core")
    xl = lax.axis_index("xl")
    head = head_slot()

    def shifted_block(q, ref, u, state):
        most, total, summed = state
        scores = lax.dot_general(q, span_keys(ref, u), NT, preferred_element_type=jnp.float32) * SCALE
        newest = jnp.maximum(most, jnp.max(scores, axis=1, keepdims=True))
        weight = jnp.exp(scores - newest)
        factor = jnp.exp(most - newest)
        total = total * factor + jnp.sum(weight, axis=1, keepdims=True)
        added = jnp.dot(weight.astype(jnp.bfloat16), span_values(ref, u), preferred_element_type=jnp.float32)
        return newest, total, summed * factor + added

    def shifted_span(t, carry):
        q = q_rows(own_ref, t)
        state = (
            jnp.full((Q_ROWS, 1), -1e30, jnp.float32),
            jnp.zeros((Q_ROWS, 1), jnp.float32),
            jnp.zeros((Q_ROWS, D), jnp.float32),
        )
        low, high = own_range(mask_ref, core, t)
        state = lax.fori_loop(low, high, lambda u, s: shifted_block(q, own_ref, u, s), state)
        low, high = peer_range(mask_ref, core, t)
        state = lax.fori_loop(low, high, lambda u, s: shifted_block(q, peer_ref, u, s), state)
        _, total, summed = state
        out_ref[pl.ds(t * 8, 8), 0:HALF, :] = (summed / total).astype(jnp.bfloat16).reshape(8, HALF, D)
        return carry

    @pl.when(head < HEADS)
    def _():
        acc_ref[...] = acc_in[...]
        tot_ref[...] = tot_in[...]
        accumulate(lambda t: peer_range(mask_ref, core, t), own_ref, peer_ref, acc_ref, tot_ref, list_ref)
        least = jnp.full((Q_ROWS, 1), 1.0, jnp.float32)
        largest = least
        for t in range(8):
            total = jnp.sum(tot_ref[t], axis=1, keepdims=True)
            least = jnp.minimum(least, total)
            largest = jnp.maximum(largest, total)
            attn = acc_ref[t] * (1.0 / total)
            out_ref[t * 8 : (t + 1) * 8, 0:HALF, :] = attn.astype(jnp.bfloat16).reshape(8, HALF, D)
        sound = jnp.logical_and(jnp.min(least) >= LEAST, jnp.max(largest) <= LARGEST)

        @pl.when(jnp.logical_not(sound))
        def _():
            lax.fori_loop(0, 8, shifted_span, 0)

        fin = fin_ref[0]
        column = head // 3
        start = core * HALF + xl * (HALF // 2)

        def commit(ref):
            for t in range(8):
                slot = (fin // 2) * 8 + t
                for i in range(2):
                    rows = ref[slot, pl.ds(pl.multiple_of(start + i * TOK, 16), HALF // 2), :]
                    out_ref[t * 8 + column, pl.ds(HALF + i * (HALF // 2), HALF // 2), :] = rows

        pl.when(fin % 2 == core)(lambda: commit(own_ref))
        pl.when(fin % 2 != core)(lambda: commit(peer_ref))


def finish_kernel(step_ref, in_ref, gate_ref, mixed_ref, k_ref, v_ref):
    gate = gate_ref[pl.ds(step_ref[0], 1), :]
    for h in range(HEADS):
        cols = slice(h * D, (h + 1) * D)
        for x in range(2):
            rows = slice(x * HALF, (x + 1) * HALF)
            attn = in_ref[x * SLOTS + h, 0:HALF, :].astype(jnp.float32)
            mixed_ref[0, rows, cols] = (attn * gate[:, cols]).astype(jnp.bfloat16)
    patch = patch_index()
    for i in range(3):
        for x in range(2):
            src = x * SLOTS + 3 * patch + i
            rows = slice(x * (HALF // 2), (x + 1) * (HALF // 2))
            k_ref[rows, i * D : (i + 1) * D] = in_ref[src, HALF : HALF + HALF // 2, :]
            v_ref[rows, i * D : (i + 1) * D] = in_ref[src, HALF + HALF // 2 : OUT_ROWS, :]


PARAMS = pltpu.CompilerParams(vmem_limit_bytes=32 * 1024 * 1024)


def on_device(queries, keys, values, q_gain, k_gain, gate_table, noise_step, block_mask, finished):
    bf16 = jnp.bfloat16
    f32 = jnp.float32
    packed = pl.pallas_call(
        pack_kernel,
        out_shape=jax.ShapeDtypeStruct((CHIPS, ROWS, D), bf16),
        in_specs=[HBM] * 5,
        out_specs=VMEM,
        scratch_shapes=[pltpu.VMEM((1, TOK, HD), bf16)] * 3
        + [pltpu.VMEM((HEADS, D), f32)] * 2
        + [pltpu.SemaphoreType.DMA((5,))],
        compiler_params=pltpu.CompilerParams(vmem_limit_bytes=60 * 1024 * 1024),
    )(queries, keys, values, q_gain.reshape(HEADS, D), k_gain.reshape(HEADS, D))
    own = lax.all_to_all(packed, PLANE, 0, 0, tiled=True)
    peer = lax.ppermute(own, "core", [(0, 1), (1, 0)])
    sums = [jax.ShapeDtypeStruct((9, Q_ROWS, D), f32)] * 2
    blocks = pltpu.SMEM((3, 64), jnp.int32)
    acc, tot = pl.pallas_call(
        own_kernel,
        out_shape=sums,
        in_specs=[SMEM, VMEM],
        out_specs=[VMEM, VMEM],
        scratch_shapes=[blocks],
        compiler_params=PARAMS,
        cost_estimate=pl.CostEstimate(flops=2**31, bytes_accessed=2**22, transcendentals=2**22),
    )(block_mask, own)
    outs = pl.pallas_call(
        peer_kernel,
        out_shape=jax.ShapeDtypeStruct((CHIPS, OUT_ROWS, D), bf16),
        in_specs=[SMEM, SMEM, VMEM, VMEM, VMEM, VMEM],
        out_specs=VMEM,
        scratch_shapes=[pltpu.VMEM((9, Q_ROWS, D), f32)] * 2 + [blocks],
        compiler_params=PARAMS,
    )(block_mask, finished, own, peer, acc, tot)
    back = lax.all_to_all(outs, PLANE, 0, 0, tiled=True)
    return pl.pallas_call(
        finish_kernel,
        out_shape=(
            jax.ShapeDtypeStruct((1, TOK, HD), bf16),
            jax.ShapeDtypeStruct((HALF, 3 * D), bf16),
            jax.ShapeDtypeStruct((HALF, 3 * D), bf16),
        ),
        in_specs=[SMEM, VMEM, VMEM],
        out_specs=(VMEM, VMEM, VMEM),
        compiler_params=PARAMS,
    )(noise_step, back, gate_table)


def solution(mesh):
    fine = Mesh(mesh.devices.reshape(2, 4, 2, 2, 4), ("xl", "y", "core", "xh", "z"))
    span, patch = ("xl", "y", "core"), ("xh", "z")
    rows = P(span, patch, None)
    return jax.shard_map(
        on_device,
        mesh=fine,
        in_specs=(rows, rows, rows, P(), P(), P(), P(span), P(), P()),
        out_specs=(rows, P(span, patch), P(span, patch)),
        check_vma=False,
    )
```

time: 109 us -> 111 us (1.018)
  the two profiles are of different devices: /device:TPU:1 before, /device:TPU:0 now
where the time goes in v1:
time: 111 us; the launch traced here: 109 us
  blocking collectives  47.9 us (43%)
  Pallas kernels  40.8 us (37%)
  waiting for transfers between devices  13.3 us (12%)
  starting transfers between devices  4.65 us (4%)
  between operations  1.99 us (2%)
    all_to_all x1, blocking collectives, on_device(): own = lax.all_to_all(packed, PLANE, 0, 0, tiled=True)  47.9 us
    pallas_call x1, Pallas kernels, on_device(): pl.pallas_call(peer_kernel, out_shape=jax.ShapeDtypeStruct((CHIPS, OUT_RO...  29.3 us
    all_to_all x1, waiting for transfers between devices, on_device(): back = lax.all_to_all(outs, PLANE, 0, 0, tiled=True)  13.3 us
    pallas_call x1, Pallas kernels, on_device(): pl.pallas_call(own_kernel, out_shape=sums, in_specs=[SMEM, VMEM], out_spe...  7.55 us
    all_to_all x1, starting transfers between devices, on_device(): back = lax.all_to_all(outs, PLANE, 0, 0, tiled=True)  4.65 us
    pallas_call x1, Pallas kernels, on_device(): pl.pallas_call(pack_kernel, out_shape=jax.ShapeDtypeStruct((CHIPS, ROWS,...  3.11 us
  transfers between devices with their start and end apart: 2, of which 1 were waited for; matrix products, arithmetic and copies ran while one was open for 0% of the time, Pallas kernels for 7%

profile of v1, /device:TPU:0, one launch (start us, length us, event | category | flops | bytes accessed | tf_op | source)
XLA Modules:
  0.0 108.7 jit_solution(15177787355445195949)
XLA Ops:
  0.6 3.1 %shard_map.112 = bf16[64,160,128]{2,1,0:T(8,128)(2,1)} custom-call(bf16[1,64,3072]{2,1,0:T(8,128)(2,1)} %q_hbm.1, bf16[1,64,3072]{2,1,0:T(8,128)(2,1)} %k_hbm.1, bf16[1,64,3072]{2,1,0:T(8,128)(2,1)} %v_hbm.1, f32[24,128]{1,0:T(8,128)} %bitcast.2, f32[24,128]{1,0:T(8,128)} %bitcast.3), custom_call_target="tpu_custom_call" | custom-call | tf_op jit(solution)/shard_map/pallas_call | solution.py:238
  3.8 0.0 copy-start.1
  3.8 47.9 %all_to_all.10.own_ref = bf16[64,160,128]{2,1,0:T(8,128)(2,1)S(1)} all-to-all(bf16[64,160,128]{2,1,0:T(8,128)(2,1)} %shard_map.112), channel_id=1, replica_groups=mesh['xl'=2,'y'=4,'core'=2,'xh'=2,'z'=4] {'xl','y','xh','z'}, dimensions={0} | all-to-all | bytes 5242880 | tf_op jit(solution)/shard_map/all_to_all | solution.py:248
  51.7 0.0 collective-permute-start
  52.3 0.0 copy-done.1
  52.3 7.5 %shard_map.113 = (f32[9,256,128]{2,1,0:T(8,128)S(1)}, f32[9,256,128]{2,1,0:T(8,128)S(1)}) custom-call(s32[16,16]{1,0:T(8,128)S(1)} %copy-done.1, bf16[64,160,128]{2,1,0:T(8,128)(2,1)S(1)} %all_to_all.10.own_ref), custom_call_target="tpu_custom_call" | custom-call | flops 2147483648 | bytes 4194304 | tf_op jit(solution)/shard_map/pallas_call | solution.py:252
  59.9 0.0 collective-permute-done.peer_ref
  59.9 0.0 copy-start
  59.9 29.3 %shard_map.114 = bf16[64,64,128]{2,1,0:T(8,128)(2,1)} custom-call(s32[16,16]{1,0:T(8,128)S(1)} %copy-done.1, s32[1]{0:T(128)S(6)} %copy.13.fin_ref, bf16[64,160,128]{2,1,0:T(8,128)(2,1)S(1)} %all_to_all.10.own_ref, bf16[64,160,128]{2,1,0:T(8,128)(2,1)S(1)} %collective-permute-done.peer_ref, f32[9,256,128]{2,1,0:T(8,128)S(1)} %get-tuple-element.5.acc_in, ...), custom_call_target="tpu_custom_call" | custom-call | tf_op jit(solution)/shard_map/pallas_call | solution.py:261
  89.2 4.7 %all-to-all-start.1 = ((bf16[64,64,128]{2,1,0:T(8,128)(2,1)}), bf16[64,64,128]{2,1,0:T(8,128)(2,1)S(1)}, u32[]{:S(2)}, u32[]{:S(2)}) async-start(bf16[64,64,128]{2,1,0:T(8,128)(2,1)} %shard_map.114), calls=%async_computation.1 | async-start | bytes 2097152 | tf_op jit(solution)/shard_map/all_to_all | solution.py:269
  94.5 13.3 %all-to-all-done.1.in_ref = bf16[64,64,128]{2,1,0:T(8,128)(2,1)S(1)} async-done(((bf16[64,64,128]{2,1,0:T(8,128)(2,1)}), bf16[64,64,128]{2,1,0:T(8,128)(2,1)S(1)}, u32[]{:S(2)}, u32[]{:S(2)}) %all-to-all-start.1) | async-done | bytes 1048608 | tf_op jit(solution)/shard_map/all_to_all | solution.py:269
  107.8 0.0 copy-done
  107.8 0.8 shard_map.115
Async XLA Ops:
  3.8 48.6 %copy-start.1 = (s32[16,16]{1,0:T(8,128)S(1)}, s32[16,16]{1,0:T(8,128)}, u32[]{:S(2)}) copy-start(s32[16,16]{1,0:T(8,128)} %mask_ref.3) | copy-start | bytes 3076
  51.7 8.2 %collective-permute-start = (bf16[64,160,128]{2,1,0:T(8,128)(2,1)S(1)}, bf16[64,160,128]{2,1,0:T(8,128)(2,1)S(1)}, u32[]{:S(2)}, u32[]{:S(2)}) collective-permute-start(bf16[64,160,128]{2,1,0:T(8,128)(2,1)S(1)} %all_to_all.10.own_ref), channel_id=1, source_target_pairs={{0,8},{8,0},{1,9},{9,1},{2,10},{10,2},{3,11},{11,3},{4,12},{12,4},... | collective-permute-start | bytes 7864328 | tf_op jit(solution)/shard_map/ppermute | solution.py:249
  59.9 47.9 %copy-start = (f32[50,3072]{1,0:T(8,128)S(1)}, f32[50,3072]{1,0:T(8,128)}, u32[]{:S(2)}) copy-start(f32[50,3072]{1,0:T(8,128)} %gate_ref.1) | copy-start | bytes 1843204
  89.2 18.6 %all-to-all-start.1 = ((bf16[64,64,128]{2,1,0:T(8,128)(2,1)}), bf16[64,64,128]{2,1,0:T(8,128)(2,1)S(1)}, u32[]{:S(2)}, u32[]{:S(2)}) async-start(bf16[64,64,128]{2,1,0:T(8,128)(2,1)} %shard_map.114), calls=%async_computation.1 | async-start | bytes 2097152 | tf_op jit(solution)/shard_map/all_to_all | solution.py:269

commit v2 on v1

--- a/solution.py
+++ b/solution.py
@@ -17,16 +17,20 @@
 SLOTS = 32
 CHIPS = 2 * SLOTS
 ROWS = 2 * TOK + HALF
-OUT_ROWS = 2 * HALF
+SPARE = 12
+PART = HALF // 2
+SPARE_ROWS = 8 * PART
 PLANE = ("xl", "y", "xh", "z")
 EPS = 1e-06
 SCALE = D ** (-0.5)
 SCALE_LOG2 = SCALE * math.log2(math.e)
 Q_ROWS = 8 * HALF
+GROUP = 4
 BATCH = 4
 LEAST, LARGEST = 2.0**-60, 2.0**100
 NT = (((1,), (1,)), ((), ()))
 VMEM = pl.BlockSpec(memory_space=pltpu.VMEM)
+ANY = pl.BlockSpec(memory_space=pl.ANY)
 HBM = pl.BlockSpec(memory_space=pltpu.HBM)
 SMEM = pl.BlockSpec(memory_space=pltpu.SMEM)
 
@@ -39,37 +43,91 @@
     return lax.axis_index("xh") * 4 + lax.axis_index("z")
 
 
-def pack_kernel(q_hbm, k_hbm, v_hbm, qg_hbm, kg_hbm, out_ref, q_ref, k_ref, v_ref, q_gain, k_gain, sems):
+def normed(ref, scale, gain, h):
+    wide = ref[:, h * D : (h + 1) * D].astype(jnp.float32)
+    return (wide * scale * gain[h : h + 1, :]).astype(jnp.bfloat16)
+
+
+def norm_factor(ref):
+    wide = ref[...].astype(jnp.float32)
+    return lax.rsqrt(jnp.mean(wide * wide, axis=-1, keepdims=True) + EPS)
+
+
+def pack_kernel(q_hbm, k_hbm, v_hbm, qg_hbm, kg_hbm, out_hbm, q_ref, k_ref, v_ref, q_gain, k_gain, out_ref, sems, out_sems):
     copies = [
         pltpu.make_async_copy(src, dst, sems.at[i])
         for i, (src, dst) in enumerate(
-            ((q_hbm, q_ref), (k_hbm, k_ref), (v_hbm, v_ref), (qg_hbm, q_gain), (kg_hbm, k_gain))
+            ((q_hbm.at[0], q_ref), (k_hbm.at[0], k_ref), (v_hbm.at[0], v_ref), (qg_hbm, q_gain), (kg_hbm, k_gain))
         )
     ]
     for copy in copies:
         copy.start()
-
-    def factor(ref):
-        wide = ref[0].astype(jnp.float32)
-        return lax.rsqrt(jnp.mean(wide * wide, axis=-1, keepdims=True) + EPS)
-
-    def normed(ref, scale, gain, h):
-        wide = ref[0, :, h * D : (h + 1) * D].astype(jnp.float32)
-        return (wide * scale * gain[h : h + 1, :]).astype(jnp.bfloat16)
-
     copies[0].wait()
-    q_factor = factor(q_ref)
+    q_factor = norm_factor(q_ref)
     copies[1].wait()
-    k_factor = factor(k_ref)
+    k_factor = norm_factor(k_ref)
     for copy in copies[2:]:
         copy.wait()
+    sent = []
     for h in range(HEADS):
         qn = normed(q_ref, q_factor, q_gain, h)
         kn = normed(k_ref, k_factor, k_gain, h)
         for x in range(2):
             out_ref[x * SLOTS + h, 0:TOK, :] = kn
-            out_ref[x * SLOTS + h, TOK : 2 * TOK, :] = v_ref[0, :, h * D : (h + 1) * D]
+            out_ref[x * SLOTS + h, TOK : 2 * TOK, :] = v_ref[:, h * D : (h + 1) * D]
             out_ref[x * SLOTS + h, 2 * TOK : ROWS, :] = qn[x * HALF : (x + 1) * HALF]
+        if h % GROUP == GROUP - 1:
+            for x in range(2):
+                group = pl.ds(x * SLOTS + h + 1 - GROUP, GROUP)
+                sent.append(pltpu.make_async_copy(out_ref.at[group], out_hbm.at[group], out_sems.at[len(sent)]))
+                sent[-1].start()
+    for copy in sent:
+        copy.wait()
+
+
+def spare_kernel(fin_ref, k_own, v_own, k_peer, v_peer, kg_hbm, packed, out_hbm, k_ref, v_ref, k_gain, stage, sems):
+    fin = fin_ref[0]
+    core = lax.axis_index("core")
+    rows = pl.ds(pl.multiple_of(core * HALF, HALF), HALF)
+
+    @pl.when(fin // 2 == lax.axis_index("xl") * 4 + lax.axis_index("y"))
+    def _():
+        def fetch(k_hbm, v_hbm):
+            copies = [
+                pltpu.make_async_copy(src, dst, sems.at[i])
+                for i, (src, dst) in enumerate(((k_hbm.at[0, rows], k_ref), (v_hbm.at[0, rows], v_ref), (kg_hbm, k_gain)))
+            ]
+            for copy in copies:
+                copy.start()
+            for copy in copies:
+                copy.wait()
+
+        pl.when(fin % 2 == core)(lambda: fetch(k_own, v_own))
+        pl.when(fin % 2 != core)(lambda: fetch(k_peer, v_peer))
+        factor = norm_factor(k_ref)
+        for p in range(8):
+            for i in range(3):
+                h = 3 * p + i
+                kn = normed(k_ref, factor, k_gain, h)
+                vn = v_ref[:, h * D : (h + 1) * D]
+                for half in range(2):
+                    part = slice(half * PART, (half + 1) * PART)
+                    stage[i * 4 + half, p * PART : (p + 1) * PART, :] = kn[part]
+                    stage[i * 4 + 2 + half, p * PART : (p + 1) * PART, :] = vn[part]
+        copies = [
+            pltpu.make_async_copy(stage.at[pl.ds(0, 8)], out_hbm.at[pl.ds(HEADS, 8), pl.ds(0, SPARE_ROWS)], sems.at[3]),
+            pltpu.make_async_copy(
+                stage.at[pl.ds(8, SPARE - 8)], out_hbm.at[pl.ds(SLOTS + HEADS, SPARE - 8), pl.ds(0, SPARE_ROWS)], sems.at[4]
+            ),
+        ]
+        for copy in copies:
+            copy.start()
+        for copy in copies:
+            copy.wait()
+
+
+def spare_slot(e):
+    return HEADS + e if e < 8 else SLOTS + HEADS + e - 8
 
 
 def q_rows(ref, t):
@@ -197,19 +255,12 @@
         def _():
             lax.fori_loop(0, 8, shifted_span, 0)
 
+    @pl.when(jnp.logical_and(head >= HEADS, xl * 8 + head - HEADS < SPARE))
+    def _():
         fin = fin_ref[0]
-        column = head // 3
-        start = core * HALF + xl * (HALF // 2)
-
-        def commit(ref):
-            for t in range(8):
-                slot = (fin // 2) * 8 + t
-                for i in range(2):
-                    rows = ref[slot, pl.ds(pl.multiple_of(start + i * TOK, 16), HALF // 2), :]
-                    out_ref[t * 8 + column, pl.ds(HALF + i * (HALF // 2), HALF // 2), :] = rows
-
-        pl.when(fin % 2 == core)(lambda: commit(own_ref))
-        pl.when(fin % 2 != core)(lambda: commit(peer_ref))
+        for t in range(8):
+            for p in range(8):
+                out_ref[t * 8 + p, 0:PART, :] = own_ref[(fin // 2) * 8 + t, p * PART : (p + 1) * PART, :]
 
 
 def finish_kernel(step_ref, in_ref, gate_ref, mixed_ref, k_ref, v_ref):
@@ -220,33 +271,48 @@
             rows = slice(x * HALF, (x + 1) * HALF)
             attn = in_ref[x * SLOTS + h, 0:HALF, :].astype(jnp.float32)
             mixed_ref[0, rows, cols] = (attn * gate[:, cols]).astype(jnp.bfloat16)
-    patch = patch_index()
-    for i in range(3):
-        for x in range(2):
-            src = x * SLOTS + 3 * patch + i
-            rows = slice(x * (HALF // 2), (x + 1) * (HALF // 2))
-            k_ref[rows, i * D : (i + 1) * D] = in_ref[src, HALF : HALF + HALF // 2, :]
-            v_ref[rows, i * D : (i + 1) * D] = in_ref[src, HALF + HALF // 2 : OUT_ROWS, :]
+    for e in range(SPARE):
+        i, half = e // 4, e % 2
+        ref = k_ref if e % 4 < 2 else v_ref
+        ref[half * PART : (half + 1) * PART, i * D : (i + 1) * D] = in_ref[spare_slot(e), 0:PART, :]
 
 
 PARAMS = pltpu.CompilerParams(vmem_limit_bytes=32 * 1024 * 1024)
+
+WIDE = pltpu.CompilerParams(vmem_limit_bytes=60 * 1024 * 1024)
 
 
 def on_device(queries, keys, values, q_gain, k_gain, gate_table, noise_step, block_mask, finished):
     bf16 = jnp.bfloat16
     f32 = jnp.float32
+    gain = k_gain.reshape(HEADS, D)
+    swap = [(0, 1), (1, 0)]
+    k_peer = lax.ppermute(keys, "core", swap)
+    v_peer = lax.ppermute(values, "core", swap)
     packed = pl.pallas_call(
         pack_kernel,
         out_shape=jax.ShapeDtypeStruct((CHIPS, ROWS, D), bf16),
         in_specs=[HBM] * 5,
-        out_specs=VMEM,
-        scratch_shapes=[pltpu.VMEM((1, TOK, HD), bf16)] * 3
+        out_specs=HBM,
+        scratch_shapes=[pltpu.VMEM((TOK, HD), bf16)] * 3
         + [pltpu.VMEM((HEADS, D), f32)] * 2
-        + [pltpu.SemaphoreType.DMA((5,))],
-        compiler_params=pltpu.CompilerParams(vmem_limit_bytes=60 * 1024 * 1024),
-    )(queries, keys, values, q_gain.reshape(HEADS, D), k_gain.reshape(HEADS, D))
+        + [pltpu.VMEM((CHIPS, ROWS, D), bf16)]
+        + [pltpu.SemaphoreType.DMA((5,)), pltpu.SemaphoreType.DMA((2 * HEADS // GROUP,))],
+        compiler_params=WIDE,
+        cost_estimate=pl.CostEstimate(flops=2**24, bytes_accessed=2**23, transcendentals=0),
+    )(queries, keys, values, q_gain.reshape(HEADS, D), gain)
+    packed = pl.pallas_call(
+        spare_kernel,
+        out_shape=jax.ShapeDtypeStruct((CHIPS, ROWS, D), bf16),
+        in_specs=[SMEM, HBM, HBM, ANY, ANY, HBM, HBM],
+        out_specs=HBM,
+        scratch_shapes=[pltpu.VMEM((HALF, HD), bf16)] * 2
+        + [pltpu.VMEM((HEADS, D), f32), pltpu.VMEM((SPARE, SPARE_ROWS, D), bf16), pltpu.SemaphoreType.DMA((5,))],
+        input_output_aliases={6: 0},
+        compiler_params=pltpu.CompilerParams(vmem_limit_bytes=48 * 1024 * 1024),
+    )(finished, keys, values, k_peer, v_peer, gain, packed)
     own = lax.all_to_all(packed, PLANE, 0, 0, tiled=True)
-    peer = lax.ppermute(own, "core", [(0, 1), (1, 0)])
+    peer = lax.ppermute(own, "core", swap)
     sums = [jax.ShapeDtypeStruct((9, Q_ROWS, D), f32)] * 2
     blocks = pltpu.SMEM((3, 64), jnp.int32)
     acc, tot = pl.pallas_call(
@@ -260,7 +326,7 @@
     )(block_mask, own)
     outs = pl.pallas_call(
         peer_kernel,
-        out_shape=jax.ShapeDtypeStruct((CHIPS, OUT_ROWS, D), bf16),
+        out_shape=jax.ShapeDtypeStruct((CHIPS, HALF, D), bf16),
         in_specs=[SMEM, SMEM, VMEM, VMEM, VMEM, VMEM],
         out_specs=VMEM,
         scratch_shapes=[pltpu.VMEM((9, Q_ROWS, D), f32)] * 2 + [blocks],

time: 111 us -> 111 us (level); the launches traced: 109 us -> 113 us
  Pallas kernels: 40.8 us -> 44.3 us
  waiting for transfers between devices: 13.3 us -> 10.9 us
  local copies, waits for them, and re-layouts: 0.01 us -> 1.76 us
    pallas_call x1 -> x2, Pallas kernels: 29.3 us -> 32.1 us  [the longest x1 32.1 us: on_device(): pl.pallas_call(peer_kernel, out_shape=jax.ShapeDtypeStruct((CHIPS, HALF,...]
    all_to_all x1, waiting for transfers between devices: 13.3 us -> 10.9 us  [on_device(): back = lax.all_to_all(outs, PLANE, 0, 0, tiled=True)]
    unnamed x4 -> x12, local copies, waits for them, and re-layouts: 0.01 us -> 1.76 us
  transfers between devices with their start and end apart: 2 -> 4, of which waited for: 1 -> 1; matrix products, arithmetic and copies ran while one was open for 0% -> 0% of each run, Pallas kernels for 7% -> 10%
where the time goes in v2:
time: 111 us; the launch traced here: 113 us
  blocking collectives  48.8 us (44%)
  Pallas kernels  44.3 us (40%)
  waiting for transfers between devices  10.9 us (10%)
  starting transfers between devices  5.22 us (5%)
  between operations  2.07 us (2%)
  local copies, waits for them, and re-layouts  1.76 us (2%)
    all_to_all x1, blocking collectives, on_device(): own = lax.all_to_all(packed, PLANE, 0, 0, tiled=True)  48.8 us
    pallas_call x1, Pallas kernels, on_device(): pl.pallas_call(peer_kernel, out_shape=jax.ShapeDtypeStruct((CHIPS, HALF,...  32.1 us
    all_to_all x1, waiting for transfers between devices, on_device(): back = lax.all_to_all(outs, PLANE, 0, 0, tiled=True)  10.9 us
    pallas_call x1, Pallas kernels, on_device(): pl.pallas_call(own_kernel, out_shape=sums, in_specs=[SMEM, VMEM], out_spe...  8.59 us
    all_to_all x1, starting transfers between devices, on_device(): back = lax.all_to_all(outs, PLANE, 0, 0, tiled=True)  4.63 us
    pallas_call x1, Pallas kernels, on_device(): pl.pallas_call(pack_kernel, out_shape=jax.ShapeDtypeStruct((CHIPS, ROWS,...  2.78 us
  transfers between devices with their start and end apart: 4, of which 1 were waited for; matrix products, arithmetic and copies ran while one was open for 0% of the time, Pallas kernels for 10%

profile of v2, /device:TPU:0, one launch (start us, length us, event | category | flops | bytes accessed | tf_op | source)
XLA Modules:
  0.0 113.1 jit_solution(3803217374718196040)
XLA Ops:
  0.6 0.0 copy-start.1
  0.6 0.0 copy-start.2
  0.7 0.0 copy-start.4
  0.7 0.1 collective-permute-start
  0.8 0.5 collective-permute-start.1
  1.9 2.8 %shard_map.112.packed = bf16[64,160,128]{2,1,0:T(8,128)(2,1)} custom-call(bf16[1,64,3072]{2,1,0:T(8,128)(2,1)} %q_hbm.1, bf16[1,64,3072]{2,1,0:T(8,128)(2,1)} %k_own.1, bf16[1,64,3072]{2,1,0:T(8,128)(2,1)} %v_own.1, f32[24,128]{1,0:T(8,128)} %bitcast.4, f32[24,128]{1,0:T(8,128)} %bitcast.2), custom_call_target="tpu_custom_call" | custom-call | flops 16777216 | bytes 8388608 | tf_op jit(solution)/shard_map/pallas_call | solution.py:292
  4.7 0.0 collective-permute-done.k_peer
  4.7 0.0 collective-permute-done.1.v_peer
  4.7 0.0 copy-done.1
  4.7 0.0 copy-done.2
  4.7 0.0 copy-done.4
  4.7 0.0 copy-start
  4.8 1.7 %copy-done = bf16[64,160,128]{2,1,0:T(8,128)(2,1)S(1)} copy-done((bf16[64,160,128]{2,1,0:T(8,128)(2,1)S(1)}, bf16[64,160,128]{2,1,0:T(8,128)(2,1)}, u32[]{:S(2)}) %copy-start) | copy-done | bytes 2621464
  6.5 0.0 copy-start.5
  6.6 48.8 %all_to_all.10.own_ref = bf16[64,160,128]{2,1,0:T(8,128)(2,1)S(1)} all-to-all(bf16[64,160,128]{2,1,0:T(8,128)(2,1)S(1)} %shard_map.113), channel_id=1, replica_groups=mesh['xl'=2,'y'=4,'core'=2,'xh'=2,'z'=4] {'xl','y','xh','z'}, dimensions={0} | all-to-all | bytes 5242880 | tf_op jit(solution)/shard_map/all_to_all | solution.py:314
  55.4 0.0 collective-permute-start.2
  55.4 0.0 copy-done.5
  55.4 8.6 %shard_map.114 = (f32[9,256,128]{2,1,0:T(8,128)S(1)}, f32[9,256,128]{2,1,0:T(8,128)S(1)}) custom-call(s32[16,16]{1,0:T(8,128)S(1)} %copy-done.5, bf16[64,160,128]{2,1,0:T(8,128)(2,1)S(1)} %all_to_all.10.own_ref), custom_call_target="tpu_custom_call" | custom-call | flops 2147483648 | bytes 4194304 | tf_op jit(solution)/shard_map/pallas_call | solution.py:318
  64.0 0.0 collective-permute-done.2.peer_ref
  64.0 0.0 copy-start.3
  64.0 32.1 %shard_map.115 = bf16[64,32,128]{2,1,0:T(8,128)(2,1)} custom-call(s32[16,16]{1,0:T(8,128)S(1)} %copy-done.5, s32[1]{0:T(128)S(6)} %copy.15.fin_ref, bf16[64,160,128]{2,1,0:T(8,128)(2,1)S(1)} %all_to_all.10.own_ref, bf16[64,160,128]{2,1,0:T(8,128)(2,1)S(1)} %collective-permute-done.2.peer_ref, f32[9,256,128]{2,1,0:T(8,128)S(1)} %get-tuple-element.5.acc_in, ...), custom_call_target="tpu_custom_call" | custom-call | tf_op jit(solution)/shard_map/pallas_call | solution.py:327
  96.1 4.6 %all-to-all-start.1 = ((bf16[64,32,128]{2,1,0:T(8,128)(2,1)}), bf16[64,32,128]{2,1,0:T(8,128)(2,1)S(1)}, u32[]{:S(2)}, u32[]{:S(2)}) async-start(bf16[64,32,128]{2,1,0:T(8,128)(2,1)} %shard_map.115), calls=%async_computation.1 | async-start | bytes 1048576 | tf_op jit(solution)/shard_map/all_to_all | solution.py:335
  101.4 10.9 %all-to-all-done.1.in_ref = bf16[64,32,128]{2,1,0:T(8,128)(2,1)S(1)} async-done(((bf16[64,32,128]{2,1,0:T(8,128)(2,1)}), bf16[64,32,128]{2,1,0:T(8,128)(2,1)S(1)}, u32[]{:S(2)}, u32[]{:S(2)}) %all-to-all-start.1) | async-done | bytes 524320 | tf_op jit(solution)/shard_map/all_to_all | solution.py:335
  112.2 0.8 shard_map.116
  (2 shorter events, 0.0 us)
Async XLA Ops:
  0.6 4.1 %copy-start.1 = (bf16[1,64,3072]{2,1,0:T(8,128)(2,1)S(1)}, bf16[1,64,3072]{2,1,0:T(8,128)(2,1)}, u32[]{:S(2)}) copy-start(bf16[1,64,3072]{2,1,0:T(8,128)(2,1)} %k_own.1) | copy-start | bytes 1179652
  0.6 4.1 %copy-start.2 = (bf16[1,64,3072]{2,1,0:T(8,128)(2,1)S(1)}, bf16[1,64,3072]{2,1,0:T(8,128)(2,1)}, u32[]{:S(2)}) copy-start(bf16[1,64,3072]{2,1,0:T(8,128)(2,1)} %v_own.1) | copy-start | bytes 1179652
  0.7 4.1 %copy-start.4 = (f32[3072]{0:T(1024)S(1)}, f32[3072]{0:T(1024)}, u32[]{:S(2)}) copy-start(f32[3072]{0:T(1024)} %param.13) | copy-start | bytes 36868
  0.7 4.0 %collective-permute-start = (bf16[1,64,3072]{2,1,0:T(8,128)(2,1)}, bf16[1,64,3072]{2,1,0:T(8,128)(2,1)S(1)}, u32[]{:S(2)}, u32[]{:S(2)}) collective-permute-start(bf16[1,64,3072]{2,1,0:T(8,128)(2,1)} %k_own.1), channel_id=1, source_target_pairs={{0,8},{8,0},{1,9},{9,1},{2,10},{10,2},{3,11},{11,3},{4,12},{12,4},... | collective-permute-start | bytes 1179656 | tf_op jit(solution)/shard_map/ppermute | solution.py:290
  0.8 4.0 %collective-permute-start.1 = (bf16[1,64,3072]{2,1,0:T(8,128)(2,1)}, bf16[1,64,3072]{2,1,0:T(8,128)(2,1)S(1)}, u32[]{:S(2)}, u32[]{:S(2)}) collective-permute-start(bf16[1,64,3072]{2,1,0:T(8,128)(2,1)} %v_own.1), channel_id=1, source_target_pairs={{0,8},{8,0},{1,9},{9,1},{2,10},{10,2},{3,11},{11,3},{4,12},{12,4},... | collective-permute-start | bytes 1179656 | tf_op jit(solution)/shard_map/ppermute | solution.py:291
  4.7 1.7 %copy-start = (bf16[64,160,128]{2,1,0:T(8,128)(2,1)S(1)}, bf16[64,160,128]{2,1,0:T(8,128)(2,1)}, u32[]{:S(2)}) copy-start(bf16[64,160,128]{2,1,0:T(8,128)(2,1)} %shard_map.112.packed) | copy-start | bytes 7864324
  6.5 48.8 %copy-start.5 = (s32[16,16]{1,0:T(8,128)S(1)}, s32[16,16]{1,0:T(8,128)}, u32[]{:S(2)}) copy-start(s32[16,16]{1,0:T(8,128)} %mask_ref.3) | copy-start | bytes 3076
  55.4 8.6 %collective-permute-start.2 = (bf16[64,160,128]{2,1,0:T(8,128)(2,1)S(1)}, bf16[64,160,128]{2,1,0:T(8,128)(2,1)S(1)}, u32[]{:S(2)}, u32[]{:S(2)}) collective-permute-start(bf16[64,160,128]{2,1,0:T(8,128)(2,1)S(1)} %all_to_all.10.own_ref), channel_id=1, source_target_pairs={{0,8},{8,0},{1,9},{9,1},{2,10},{10,2},{3,11},{11,3},{4,12},{12,4},... | collective-permute-start | bytes 7864328 | tf_op jit(solution)/shard_map/ppermute | solution.py:315
  64.0 48.3 %copy-start.3 = (f32[50,3072]{1,0:T(8,128)S(1)}, f32[50,3072]{1,0:T(8,128)}, u32[]{:S(2)}) copy-start(f32[50,3072]{1,0:T(8,128)} %gate_ref.1) | copy-start | bytes 1843204
  96.1 16.2 %all-to-all-start.1 = ((bf16[64,32,128]{2,1,0:T(8,128)(2,1)}), bf16[64,32,128]{2,1,0:T(8,128)(2,1)S(1)}, u32[]{:S(2)}, u32[]{:S(2)}) async-start(bf16[64,32,128]{2,1,0:T(8,128)(2,1)} %shard_map.115), calls=%async_computation.1 | async-start | bytes 1048576 | tf_op jit(solution)/shard_map/all_to_all | solution.py:335

commit v3 on v1

v3 whole, which is shorter than its diff:
```python
import math

import jax
import jax.numpy as jnp
from jax import lax
from jax.experimental import pallas as pl
from jax.experimental.pallas import tpu as pltpu
from jax.sharding import Mesh
from jax.sharding import PartitionSpec as P

D = 128
HEADS = 24
HD = HEADS * D
SPANS = 16
TOK = 64
HALF = TOK // 2
SLOTS = 32
CHIPS = 2 * SLOTS
ROWS = 2 * TOK + HALF
SPARE = 12
PART = HALF // 2
PLANE = ("xl", "y", "xh", "z")
EPS = 1e-06
SCALE = D ** (-0.5)
SCALE_LOG2 = SCALE * math.log2(math.e)
Q_ROWS = 8 * HALF
BATCH = 2
LEAST, LARGEST = 2.0**-60, 2.0**100
NT = (((1,), (1,)), ((), ()))
VMEM = pl.BlockSpec(memory_space=pltpu.VMEM)
ANY = pl.BlockSpec(memory_space=pl.ANY)
SMEM = pl.BlockSpec(memory_space=pltpu.SMEM)


def head_slot():
    return lax.axis_index("y") * 8 + patch_index()


def patch_index():
    return lax.axis_index("xh") * 4 + lax.axis_index("z")


def normed(ref, rows, factor, gain, h):
    wide = ref[0, rows, h * D : (h + 1) * D].astype(jnp.float32)
    return (wide * factor * gain[h : h + 1, :]).astype(jnp.bfloat16)


def norm_factor(block):
    wide = block.astype(jnp.float32)
    return lax.rsqrt(jnp.mean(wide * wide, axis=-1, keepdims=True) + EPS)


def pack_kernel(fin_ref, q_ref, k_ref, v_ref, k_peer, v_peer, q_gain, k_gain, out_ref):
    q_factor = norm_factor(q_ref[0])
    k_factor = norm_factor(k_ref[0])
    for h in range(HEADS):
        qn = normed(q_ref, slice(None), q_factor, q_gain, h)
        kn = normed(k_ref, slice(None), k_factor, k_gain, h)
        for x in range(2):
            out_ref[x * SLOTS + h, 0:TOK, :] = kn
            out_ref[x * SLOTS + h, TOK : 2 * TOK, :] = v_ref[0, :, h * D : (h + 1) * D]
            out_ref[x * SLOTS + h, 2 * TOK : ROWS, :] = qn[x * HALF : (x + 1) * HALF]

    fin = fin_ref[0]
    core = lax.axis_index("core")
    rows = pl.ds(pl.multiple_of(core * HALF, HALF), HALF)

    def spare(k_half, v_half):
        factor = norm_factor(k_half[0, rows, :])
        for p in range(8):
            part = slice(p * PART, (p + 1) * PART)
            for i in range(3):
                h = 3 * p + i
                kn = normed(k_half, rows, factor, k_gain, h)
                vn = v_half[0, rows, h * D : (h + 1) * D]
                for half in range(2):
                    out_ref[spare_slot(i * 4 + half), part, :] = kn[half * PART : (half + 1) * PART]
                    out_ref[spare_slot(i * 4 + 2 + half), part, :] = vn[half * PART : (half + 1) * PART]

    here = fin // 2 == lax.axis_index("xl") * 4 + lax.axis_index("y")
    pl.when(jnp.logical_and(here, fin % 2 == core))(lambda: spare(k_ref, v_ref))
    pl.when(jnp.logical_and(here, fin % 2 != core))(lambda: spare(k_peer, v_peer))


def spare_slot(e):
    return HEADS + e if e < 8 else SLOTS + HEADS + e - 8


def q_rows(ref, t):
    return ref[pl.ds(t * 8, 8), 2 * TOK : ROWS, :].reshape(Q_ROWS, D)


def span_keys(ref, u, spans=1):
    return ref[pl.ds(u * 8, spans * 8), 0:TOK, :].reshape(spans * 8 * TOK, D)


def span_values(ref, u, spans=1):
    return ref[pl.ds(u * 8, spans * 8), TOK : 2 * TOK, :].reshape(spans * 8 * TOK, D)


def first_counted(mask_ref, core, t):
    c = 2 * t + core
    counted = mask_ref[c, 0]
    for j in range(1, 2 * t + 2 if isinstance(t, int) else SPANS):
        counted = counted + mask_ref[c, j]
    return c + 1 - counted


def own_range(first, core, t):
    return jnp.right_shift(first - core + 1, 1), t + 1


def peer_range(first, core, t):
    return jnp.right_shift(first + core, 1), t + core


def list_kernel(mask_any, list_ref, mask_ref, sem):
    copy = pltpu.make_async_copy(mask_any, mask_ref, sem.at[0])
    copy.start()
    core = lax.axis_index("core")
    copy.wait()
    firsts = [first_counted(mask_ref, core, t) for t in range(8)]
    for at, bounds in ((0, own_range), (4, peer_range)):
        pairs = singles = jnp.int32(0)
        for t in range(8):
            low, high = bounds(firsts[t], core, t)
            count = high - low
            list_ref[at + 2, singles] = t
            list_ref[at + 3, singles] = high - 1
            singles = singles + jnp.bitwise_and(count, 1)

            def note(i, n, t=t, low=low, at=at):
                list_ref[at, n] = t
                list_ref[at + 1, n] = low + 2 * i
                return n + 1

            pairs = lax.fori_loop(0, jnp.right_shift(count, 1), note, pairs)
        for row, total in ((at, pairs), (at + 2, singles)):
            list_ref[row, total] = 8
            list_ref[row + 1, total] = 0
            list_ref[row, 63] = total


def accumulate(list_ref, at, q_ref, kv_ref, acc_ref, tot_ref):
    def block(row, u, spans):
        q = q_rows(q_ref, jnp.minimum(row, 7))
        scores = lax.dot_general(q, span_keys(kv_ref, u, spans), NT, preferred_element_type=jnp.float32)
        weight = jnp.exp2(scores * SCALE_LOG2)
        part = weight[:, 0:D]
        for k in range(1, spans * 8 * TOK // D):
            part = part + weight[:, k * D : (k + 1) * D]
        added = jnp.dot(weight.astype(jnp.bfloat16), span_values(kv_ref, u, spans), preferred_element_type=jnp.float32)
        acc_ref[row] += added
        tot_ref[row] += part

    for spans, line in ((2, at), (1, at + 2)):

        def step(b, carry, spans=spans, line=line):
            for i in range(BATCH):
                block(list_ref[line, b * BATCH + i], list_ref[line + 1, b * BATCH + i], spans)
            return carry

        lax.fori_loop(0, (list_ref[line, 63] + BATCH - 1) // BATCH, step, 0)


def own_kernel(list_ref, own_ref, acc_ref, tot_ref):
    @pl.when(head_slot() < HEADS)
    def _():
        acc_ref[...] = jnp.zeros_like(acc_ref)
        tot_ref[...] = jnp.zeros_like(tot_ref)
        accumulate(list_ref, 0, own_ref, own_ref, acc_ref, tot_ref)


def peer_kernel(mask_any, fin_ref, list_ref, own_ref, peer_ref, acc_in, tot_in, out_ref, acc_ref, tot_ref, mask_ref, sem):
    core = lax.axis_index("core")
    xl = lax.axis_index("xl")
    head = head_slot()

    def shifted_block(q, ref, u, state):
        most, total, summed = state
        scores = lax.dot_general(q, span_keys(ref, u), NT, preferred_element_type=jnp.float32) * SCALE
        newest = jnp.maximum(most, jnp.max(scores, axis=1, keepdims=True))
        weight = jnp.exp(scores - newest)
        factor = jnp.exp(most - newest)
        total = total * factor + jnp.sum(weight, axis=1, keepdims=True)
        added = jnp.dot(weight.astype(jnp.bfloat16), span_values(ref, u), preferred_element_type=jnp.float32)
        return newest, total, summed * factor + added

    def shifted_span(t, carry):
        q = q_rows(own_ref, t)
        state = (
            jnp.full((Q_ROWS, 1), -1e30, jnp.float32),
            jnp.zeros((Q_ROWS, 1), jnp.float32),
            jnp.zeros((Q_ROWS, D), jnp.float32),
        )
        first = first_counted(mask_ref, core, t)
        low, high = own_range(first, core, t)
        state = lax.fori_loop(low, high, lambda u, s: shifted_block(q, own_ref, u, s), state)
        low, high = peer_range(first, core, t)
        state = lax.fori_loop(low, high, lambda u, s: shifted_block(q, peer_ref, u, s), state)
        _, total, summed = state
        out_ref[pl.ds(t * 8, 8), 0:HALF, :] = (summed / total).astype(jnp.bfloat16).reshape(8, HALF, D)
        return carry

    @pl.when(head < HEADS)
    def _():
        accumulate(list_ref, 4, own_ref, peer_ref, acc_ref, tot_ref)
        least = jnp.full((Q_ROWS, 1), 1.0, jnp.float32)
        largest = least
        for t in range(8):
            total = jnp.sum(tot_ref[t], axis=1, keepdims=True)
            least = jnp.minimum(least, total)
            largest = jnp.maximum(largest, total)
            attn = acc_ref[t] * (1.0 / total)
            out_ref[t * 8 : (t + 1) * 8, 0:HALF, :] = attn.astype(jnp.bfloat16).reshape(8, HALF, D)
        sound = jnp.logical_and(jnp.min(least) >= LEAST, jnp.max(largest) <= LARGEST)

        @pl.when(jnp.logical_not(sound))
        def _():
            copy = pltpu.make_async_copy(mask_any, mask_ref, sem.at[0])
            copy.start()
            copy.wait()
            lax.fori_loop(0, 8, shifted_span, 0)

    @pl.when(jnp.logical_and(head >= HEADS, xl * 8 + head - HEADS < SPARE))
    def _():
        fin = fin_ref[0]
        for t in range(8):
            for p in range(8):
                out_ref[t * 8 + p, 0:PART, :] = own_ref[(fin // 2) * 8 + t, p * PART : (p + 1) * PART, :]


def finish_kernel(step_ref, in_ref, gate_ref, mixed_ref, k_ref, v_ref):
    gate = gate_ref[pl.ds(step_ref[0], 1), :]
    for h in range(HEADS):
        cols = slice(h * D, (h + 1) * D)
        for x in range(2):
            rows = slice(x * HALF, (x + 1) * HALF)
            attn = in_ref[x * SLOTS + h, 0:HALF, :].astype(jnp.float32)
            mixed_ref[0, rows, cols] = (attn * gate[:, cols]).astype(jnp.bfloat16)
    for e in range(SPARE):
        i, half = e // 4, e % 2
        ref = k_ref if e % 4 < 2 else v_ref
        ref[half * PART : (half + 1) * PART, i * D : (i + 1) * D] = in_ref[spare_slot(e), 0:PART, :]


PARAMS = pltpu.CompilerParams(vmem_limit_bytes=32 * 1024 * 1024)


def on_device(queries, keys, values, q_gain, k_gain, gate_table, noise_step, block_mask, finished):
    bf16 = jnp.bfloat16
    f32 = jnp.float32
    swap = [(0, 1), (1, 0)]
    k_peer = lax.ppermute(keys, "core", swap)
    v_peer = lax.ppermute(values, "core", swap)
    lists = pl.pallas_call(
        list_kernel,
        out_shape=jax.ShapeDtypeStruct((8, 64), jnp.int32),
        in_specs=[ANY],
        out_specs=SMEM,
        scratch_shapes=[pltpu.SMEM((SPANS, SPANS), jnp.int32), pltpu.SemaphoreType.DMA((1,))],
        cost_estimate=pl.CostEstimate(flops=2**32, bytes_accessed=2**12, transcendentals=0),
    )(block_mask)
    k_peer, lists = lax.optimization_barrier((k_peer, lists))
    packed = pl.pallas_call(
        pack_kernel,
        out_shape=jax.ShapeDtypeStruct((CHIPS, ROWS, D), bf16),
        in_specs=[SMEM] + [VMEM] * 7,
        out_specs=VMEM,
        compiler_params=PARAMS,
    )(finished, queries, keys, values, k_peer, v_peer, q_gain.reshape(HEADS, D), k_gain.reshape(HEADS, D))
    own = lax.all_to_all(packed, PLANE, 0, 0, tiled=True)
    peer = lax.ppermute(own, "core", swap)
    sums = [jax.ShapeDtypeStruct((9, Q_ROWS, D), f32)] * 2
    acc, tot = pl.pallas_call(
        own_kernel,
        out_shape=sums,
        in_specs=[SMEM, VMEM],
        out_specs=[VMEM, VMEM],
        compiler_params=PARAMS,
        cost_estimate=pl.CostEstimate(flops=2**31, bytes_accessed=2**22, transcendentals=2**22),
    )(lists, own)
    outs, _, _ = pl.pallas_call(
        peer_kernel,
        out_shape=[jax.ShapeDtypeStruct((CHIPS, HALF, D), bf16)] + sums,
        in_specs=[ANY, SMEM, SMEM] + [VMEM] * 4,
        out_specs=[VMEM] * 3,
        scratch_shapes=[pltpu.SMEM((SPANS, SPANS), jnp.int32), pltpu.SemaphoreType.DMA((1,))],
        input_output_aliases={5: 1, 6: 2},
        compiler_params=PARAMS,
    )(block_mask, finished, lists, own, peer, acc, tot)
    back = lax.all_to_all(outs, PLANE, 0, 0, tiled=True)
    return pl.pallas_call(
        finish_kernel,
        out_shape=(
            jax.ShapeDtypeStruct((1, TOK, HD), bf16),
            jax.ShapeDtypeStruct((HALF, 3 * D), bf16),
            jax.ShapeDtypeStruct((HALF, 3 * D), bf16),
        ),
        in_specs=[SMEM, VMEM, VMEM],
        out_specs=(VMEM, VMEM, VMEM),
        compiler_params=PARAMS,
    )(noise_step, back, gate_table)


def solution(mesh):
    fine = Mesh(mesh.devices.reshape(2, 4, 2, 2, 4), ("xl", "y", "core", "xh", "z"))
    span, patch = ("xl", "y", "core"), ("xh", "z")
    rows = P(span, patch, None)
    return jax.shard_map(
        on_device,
        mesh=fine,
        in_specs=(rows, rows, rows, P(), P(), P(), P(span), P(), P()),
        out_specs=(rows, P(span, patch), P(span, patch)),
        check_vma=False,
    )
```

time: 111 us -> 104 us (0.937)
  the two profiles are of different devices: /device:TPU:0 before, /device:TPU:1 now
where the time goes in v3:
time: 104 us; the launch traced here: 106 us
  blocking collectives  46 us (44%)
  Pallas kernels  38.3 us (37%)
  waiting for transfers between devices  10.5 us (10%)
  starting transfers between devices  8.86 us (9%)
  between operations  2.1 us (2%)
    all_to_all x1, blocking collectives, on_device(): own = lax.all_to_all(packed, PLANE, 0, 0, tiled=True)  46 us
    pallas_call x1, Pallas kernels, on_device(): pl.pallas_call(peer_kernel, out_shape=[jax.ShapeDtypeStruct((CHIPS, HALF,...  29.7 us
    all_to_all x1, waiting for transfers between devices, on_device(): back = lax.all_to_all(outs, PLANE, 0, 0, tiled=True)  10.5 us
    pallas_call x1, Pallas kernels, on_device(): pl.pallas_call(own_kernel, out_shape=sums, in_specs=[SMEM, VMEM], out_spe...  5.56 us
    all_to_all x1, starting transfers between devices, on_device(): back = lax.all_to_all(outs, PLANE, 0, 0, tiled=True)  4.78 us
    ppermute x1, starting transfers between devices, on_device(): peer = lax.ppermute(own, 'core', swap)  2.49 us
  transfers between devices with their start and end apart: 4, of which 1 were waited for; matrix products, arithmetic and copies ran while one was open for 0% of the time, Pallas kernels for 7%

profile of v3, /device:TPU:1, one launch (start us, length us, event | category | flops | bytes accessed | tf_op | source)
XLA Modules:
  0.0 105.9 jit_solution(8292536358510309186)
XLA Ops:
  0.6 1.5 %collective-permute-start = (bf16[1,64,3072]{2,1,0:T(8,128)(2,1)}, bf16[1,64,3072]{2,1,0:T(8,128)(2,1)S(1)}, u32[]{:S(2)}, u32[]{:S(2)}) collective-permute-start(bf16[1,64,3072]{2,1,0:T(8,128)(2,1)} %k_ref.1), channel_id=1, source_target_pairs={{0,8},{8,0},{1,9},{9,1},{2,10},{10,2},{3,11},{11,3},{4,12},{12,4},... | collective-permute-start | bytes 1179656 | tf_op jit(solution)/shard_map/ppermute | solution.py:254
  2.1 0.1 collective-permute-start.1
  2.9 0.0 copy-start.1
  2.9 0.0 copy-start.2
  2.9 0.0 copy-start.3
  2.9 0.0 copy-start.4
  2.9 0.0 copy-start.5
  2.9 1.8 %shard_map.112.list_ref = s32[8,64]{1,0:T(8,128)} custom-call(s32[16,16]{1,0:T(8,128)} %mask_any.3), custom_call_target="tpu_custom_call" | custom-call | flops 4294967296 | bytes 4096 | tf_op jit(solution)/shard_map/pallas_call | solution.py:256
  4.8 0.0 collective-permute-done.k_peer
  4.8 0.0 collective-permute-done.1.v_peer
  4.8 0.0 copy-done.1
  4.8 0.0 copy-done.2
  4.8 0.0 copy-done.3
  4.9 0.4 shard_map.113
  5.3 0.0 copy-start.7
  5.3 46.0 %all_to_all.10.own_ref = bf16[64,160,128]{2,1,0:T(8,128)(2,1)S(1)} all-to-all(bf16[64,160,128]{2,1,0:T(8,128)(2,1)S(1)} %shard_map.113), channel_id=1, replica_groups=mesh['xl'=2,'y'=4,'core'=2,'xh'=2,'z'=4] {'xl','y','xh','z'}, dimensions={0} | all-to-all | bytes 5242880 | tf_op jit(solution)/shard_map/all_to_all | solution.py:272
  51.3 2.5 %collective-permute-start.2 = (bf16[64,160,128]{2,1,0:T(8,128)(2,1)S(1)}, bf16[64,160,128]{2,1,0:T(8,128)(2,1)S(1)}, u32[]{:S(2)}, u32[]{:S(2)}) collective-permute-start(bf16[64,160,128]{2,1,0:T(8,128)(2,1)S(1)} %all_to_all.10.own_ref), channel_id=1, source_target_pairs={{0,8},{8,0},{1,9},{9,1},{2,10},{10,2},{3,11},{11,3},{4,12},{12,4},... | collective-permute-start | bytes 7864328 | tf_op jit(solution)/shard_map/ppermute | solution.py:273
  53.8 5.6 %shard_map.114 = (f32[9,256,128]{2,1,0:T(8,128)S(1)}, f32[9,256,128]{2,1,0:T(8,128)S(1)}) custom-call(s32[8,64]{1,0:T(8,128)S(1)} %copy-done.7, bf16[64,160,128]{2,1,0:T(8,128)(2,1)S(1)} %all_to_all.10.own_ref), custom_call_target="tpu_custom_call" | custom-call | flops 2147483648 | bytes 4194304 | tf_op jit(solution)/shard_map/pallas_call | solution.py:275
  59.4 0.0 collective-permute-done.2.peer_ref
  59.4 29.7 %shard_map.115 = (bf16[64,32,128]{2,1,0:T(8,128)(2,1)}, f32[9,256,128]{2,1,0:T(8,128)S(1)}, f32[9,256,128]{2,1,0:T(8,128)S(1)}) custom-call(s32[16,16]{1,0:T(8,128)S(1)} %copy-done.6, s32[1]{0:T(128)S(6)} %copy.17.fin_ref, s32[8,64]{1,0:T(8,128)S(1)} %copy-done.7, ...), custom_call_target="tpu_custom_call", output_to_operand_aliasing={{1}: (5, {}), {2}: (6, {})} | custom-call | tf_op jit(solution)/shard_map/pallas_call | solution.py:283
  89.1 0.0 copy-start
  89.1 4.8 %all-to-all-start.1 = ((bf16[64,32,128]{2,1,0:T(8,128)(2,1)}), bf16[64,32,128]{2,1,0:T(8,128)(2,1)S(1)}, u32[]{:S(2)}, u32[]{:S(2)}) async-start(bf16[64,32,128]{2,1,0:T(8,128)(2,1)} %get-tuple-element.12), calls=%async_computation.1 | async-start | bytes 1048576 | tf_op jit(solution)/shard_map/all_to_all | solution.py:292
  94.5 10.5 %all-to-all-done.1.in_ref = bf16[64,32,128]{2,1,0:T(8,128)(2,1)S(1)} async-done(((bf16[64,32,128]{2,1,0:T(8,128)(2,1)}), bf16[64,32,128]{2,1,0:T(8,128)(2,1)S(1)}, u32[]{:S(2)}, u32[]{:S(2)}) %all-to-all-start.1) | async-done | bytes 524320 | tf_op jit(solution)/shard_map/all_to_all | solution.py:292
  105.0 0.8 shard_map.116
  (6 shorter events, 0.0 us)
Async XLA Ops:
  0.6 4.2 %collective-permute-start = (bf16[1,64,3072]{2,1,0:T(8,128)(2,1)}, bf16[1,64,3072]{2,1,0:T(8,128)(2,1)S(1)}, u32[]{:S(2)}, u32[]{:S(2)}) collective-permute-start(bf16[1,64,3072]{2,1,0:T(8,128)(2,1)} %k_ref.1), channel_id=1, source_target_pairs={{0,8},{8,0},{1,9},{9,1},{2,10},{10,2},{3,11},{11,3},{4,12},{12,4},... | collective-permute-start | bytes 1179656 | tf_op jit(solution)/shard_map/ppermute | solution.py:254
  2.1 2.7 %collective-permute-start.1 = (bf16[1,64,3072]{2,1,0:T(8,128)(2,1)}, bf16[1,64,3072]{2,1,0:T(8,128)(2,1)S(1)}, u32[]{:S(2)}, u32[]{:S(2)}) collective-permute-start(bf16[1,64,3072]{2,1,0:T(8,128)(2,1)} %v_ref.1), channel_id=1, source_target_pairs={{0,8},{8,0},{1,9},{9,1},{2,10},{10,2},{3,11},{11,3},{4,12},{12,4},... | collective-permute-start | bytes 1179656 | tf_op jit(solution)/shard_map/ppermute | solution.py:255
  2.9 1.9 %copy-start.1 = (bf16[1,64,3072]{2,1,0:T(8,128)(2,1)S(1)}, bf16[1,64,3072]{2,1,0:T(8,128)(2,1)}, u32[]{:S(2)}) copy-start(bf16[1,64,3072]{2,1,0:T(8,128)(2,1)} %q_ref.1) | copy-start | bytes 1179652
  2.9 1.9 %copy-start.2 = (bf16[1,64,3072]{2,1,0:T(8,128)(2,1)S(1)}, bf16[1,64,3072]{2,1,0:T(8,128)(2,1)}, u32[]{:S(2)}) copy-start(bf16[1,64,3072]{2,1,0:T(8,128)(2,1)} %k_ref.1) | copy-start | bytes 1179652
  2.9 1.9 %copy-start.3 = (bf16[1,64,3072]{2,1,0:T(8,128)(2,1)S(1)}, bf16[1,64,3072]{2,1,0:T(8,128)(2,1)}, u32[]{:S(2)}) copy-start(bf16[1,64,3072]{2,1,0:T(8,128)(2,1)} %v_ref.1) | copy-start | bytes 1179652
  2.9 1.9 %copy-start.4 = (f32[3072]{0:T(1024)S(1)}, f32[3072]{0:T(1024)}, u32[]{:S(2)}) copy-start(f32[3072]{0:T(1024)} %param.12) | copy-start | bytes 36868
  2.9 1.9 %copy-start.5 = (f32[3072]{0:T(1024)S(1)}, f32[3072]{0:T(1024)}, u32[]{:S(2)}) copy-start(f32[3072]{0:T(1024)} %param.13) | copy-start | bytes 36868
  5.3 48.5 %copy-start.7 = (s32[8,64]{1,0:T(8,128)S(1)}, s32[8,64]{1,0:T(8,128)}, u32[]{:S(2)}) copy-start(s32[8,64]{1,0:T(8,128)} %shard_map.112.list_ref) | copy-start | bytes 6148
  51.3 8.1 %copy-start.6 = (s32[16,16]{1,0:T(8,128)S(1)}, s32[16,16]{1,0:T(8,128)}, u32[]{:S(2)}) copy-start(s32[16,16]{1,0:T(8,128)} %mask_any.3) | copy-start | bytes 3076
  51.3 8.1 %collective-permute-start.2 = (bf16[64,160,128]{2,1,0:T(8,128)(2,1)S(1)}, bf16[64,160,128]{2,1,0:T(8,128)(2,1)S(1)}, u32[]{:S(2)}, u32[]{:S(2)}) collective-permute-start(bf16[64,160,128]{2,1,0:T(8,128)(2,1)S(1)} %all_to_all.10.own_ref), channel_id=1, source_target_pairs={{0,8},{8,0},{1,9},{9,1},{2,10},{10,2},{3,11},{11,3},{4,12},{12,4},... | collective-permute-start | bytes 7864328 | tf_op jit(solution)/shard_map/ppermute | solution.py:273
  89.1 15.9 %copy-start = (f32[50,3072]{1,0:T(8,128)S(1)}, f32[50,3072]{1,0:T(8,128)}, u32[]{:S(2)}) copy-start(f32[50,3072]{1,0:T(8,128)} %gate_ref.1) | copy-start | bytes 1843204
  89.1 15.9 %all-to-all-start.1 = ((bf16[64,32,128]{2,1,0:T(8,128)(2,1)}), bf16[64,32,128]{2,1,0:T(8,128)(2,1)S(1)}, u32[]{:S(2)}, u32[]{:S(2)}) async-start(bf16[64,32,128]{2,1,0:T(8,128)(2,1)} %get-tuple-element.12), calls=%async_computation.1 | async-start | bytes 1048576 | tf_op jit(solution)/shard_map/all_to_all | solution.py:292
